TPU v7x, 512 devices: a whole 4x8x8 slice. The times are simulated.
512 devices in a mesh: row: 16 (over y, core), col: 32 (over x, z).
Axes of the slice: x: 4, y: 8, z: 8, core: 2. Of those that a mesh axis runs over, the one named last changes fastest.
Arguments:
- logits: float32 [65536, 256], P(('row', 'col')), may hold values from -6 to 6
- tile_values: bfloat16 [16, 32, 128, 128, 128], P('row', 'col'), may hold values from -0.0625 to 0.0625
- tile_rows: int32 [16, 32, 128], P('row', 'col'), may hold values from 0 to 31, as said below
- tile_cols: int32 [16, 32, 128], P('row', 'col'), may hold values from 0 to 15, as said below
- tile_counts: int32 [16, 32], P('row', 'col'), may hold values from 16 to 128, as said below
Outputs:
- propagated: float32 [65536, 256], P(('row', 'col'))
Inputs may be any that keep to these rules, and one draw needn't show every extreme that they name: `tile_rows`: within a device's first tile_counts slots the pairs (row, column) are in ascending order, repeats possible, and block 32 - 1 of the row group meets block 16 - 1 of the column group on every device; later slots hold zeros. `tile_cols`: see tile_rows. `tile_counts`: each count is 128 divided by 1, 2, 4 or 8.
All inputs are finite; a program needn't handle non-finite values.
Results may differ from a plain program's by a relative error of at most 0.029.
Values may be sent and summed in bfloat16 or wider, within the bound.
A program may use at most 64 MiB of HBM per device.

v0:
```python
import jax
import jax.numpy as jnp
from jax import lax
from jax.sharding import PartitionSpec as P

HOPS = 2


GROUP_SLOTS = 8


def body(logits, tile_values, tile_rows, tile_cols, tile_counts):
    own_tiles = tile_values[0, 0]
    tile_row = tile_rows[0, 0]
    tile_col = tile_cols[0, 0]
    tile_total = tile_counts[0, 0]
    capacity = own_tiles.shape[0]
    tile_size = own_tiles.shape[1]
    classes = logits.shape[1]
    col_count = lax.axis_size("col")
    current = logits
    for repeat in range(HOPS):
        gathered_panel = lax.all_gather(current.astype(jnp.bfloat16), "row", axis=0, tiled=True)
        panels = gathered_panel.reshape(-1, tile_size, classes)
        rounds = capacity // GROUP_SLOTS

        def advance(turn_index, running):
            wanted = turn_index * GROUP_SLOTS
            window_start = jnp.minimum(wanted, capacity - GROUP_SLOTS)
            positions = window_start + jnp.arange(GROUP_SLOTS, dtype=jnp.int32)
            chosen = (positions >= wanted) & (positions < tile_total)
            block_tiles = lax.dynamic_slice_in_dim(own_tiles, window_start, GROUP_SLOTS, 0)
            target_rows = lax.dynamic_slice_in_dim(tile_row, window_start, GROUP_SLOTS, 0)
            source_cols = lax.dynamic_slice_in_dim(tile_col, window_start, GROUP_SLOTS, 0)
            sources = panels[source_cols]
            products = jnp.einsum(
                "gtk,gkc->gtc", block_tiles, sources, preferred_element_type=jnp.float32
            )
            products = jnp.where(chosen[:, None, None], products, jnp.float32(0.0))
            target = jnp.where(chosen, target_rows - 0, 0)
            return running.at[target].add(products)

        initial = jnp.zeros((col_count, tile_size, classes), jnp.float32)
        partial_value = lax.fori_loop(0, rounds, advance, initial)
        summed = lax.psum_scatter(
            partial_value.reshape(col_count * tile_size, classes).astype(jnp.bfloat16),
            "col",
            scatter_dimension=0,
            tiled=True,
        ).astype(jnp.float32)
        current = 0.9 * summed + 0.1 * logits
    return current


def solution(mesh):
    return jax.shard_map(
        body,
        mesh=mesh,
        in_specs=(
            P(("row", "col"), None),
            P("row", "col", None, None, None),
            P("row", "col", None),
            P("row", "col", None),
            P("row", "col"),
        ),
        out_specs=P(("row", "col"), None),
        check_vma=False,
    )
```

profile of v0, /device:TPU:1, one launch (start us, length us, event | category | flops | bytes accessed | tf_op | source)
XLA Modules:
  0.0 743.4 jit_solution(13600341799267225234)
XLA Ops:
  6.5 1.6 convert_element_type.24
  8.2 48.0 %all-gather.3.cloned.1.call-done = bf16[2048,256]{1,0:T(8,128)(2,1)} async-done(((bf16[128,256]{1,0:T(8,128)(2,1)}), bf16[2048,256]{1,0:T(8,128)(2,1)}) %all-gather.3.cloned.1.call-update) | async-done | bytes 1048592 | tf_op jit(solution)/shard_map/all_gather | solution.py:23
  56.2 2.4 broadcast.75.clone
  58.7 93.9 %while.26 = (s32[]{:T(128)}, f32[32,128,256]{2,1,0:T(8,128)}, s32[]{:T(128)}, s32[128]{0:T(128)S(1)}, bf16[128,128,128]{2,1,0:T(8,128)(2,1)}, /*index=5*/s32[128...) while((s32[]{:T(128)}, f32[32,128,256]{2,1,0:T(8,128)}, ...), condition=%wide.region_2.3_spmd, body=%wide.region_0.2_spmd.sunk | while | flops 67634272 | bytes 6033843 | solution.py:44
  61.2 3.3 scatter_fusion
  67.1 3.3 scatter_fusion
  73.0 3.3 scatter_fusion
  78.8 3.3 scatter_fusion
  84.7 3.3 scatter_fusion
  90.6 3.3 scatter_fusion
  96.5 3.3 scatter_fusion
  102.3 3.3 scatter_fusion
  107.0 1.2 convolution_select_fusion.4
  108.2 3.3 scatter_fusion
  114.1 3.3 scatter_fusion
  119.9 3.3 scatter_fusion
  125.8 3.3 scatter_fusion
  131.7 3.3 scatter_fusion
  137.6 3.3 scatter_fusion
  143.4 3.3 scatter_fusion
  148.1 1.2 convolution_select_fusion.4
  149.3 3.3 scatter_fusion
  152.6 3.8 convert_element_type.25
  156.5 215.8 %reduce-scatter.3.cloned.1.call-done = bf16[128,256]{1,0:T(8,128)(2,1)} async-done(((bf16[4096,256]{1,0:T(8,128)(2,1)}), bf16[128,256]{1,0:T(8,128)(2,1)}) %reduce-scatter.3.cloned.1.call-update) | async-done | bytes 65552 | tf_op jit(solution)/shard_map/reduce_scatter | solution.py:45
  372.3 1.5 add_convert_fusion
  373.9 45.2 %all-gather.5.cloned.1.call-done = bf16[2048,256]{1,0:T(8,128)(2,1)} async-done(((bf16[128,256]{1,0:T(8,128)(2,1)}), bf16[2048,256]{1,0:T(8,128)(2,1)}) %all-gather.5.cloned.1.call-update) | async-done | bytes 1048592 | tf_op jit(solution)/shard_map/all_gather | solution.py:23
  419.1 2.4 broadcast.75
  421.5 93.9 %while.27 = (s32[]{:T(128)}, f32[32,128,256]{2,1,0:T(8,128)}, s32[]{:T(128)}, s32[128]{0:T(128)S(1)}, bf16[128,128,128]{2,1,0:T(8,128)(2,1)}, /*index=5*/s32[128...) while((s32[]{:T(128)}, f32[32,128,256]{2,1,0:T(8,128)}, ...), condition=%wide.region_6.7_spmd, body=%wide.region_4.6_spmd.sunk | while | flops 67634272 | bytes 6033843 | solution.py:44
  424.1 3.3 scatter_fusion.1
  430.0 3.3 scatter_fusion.1
  435.8 3.3 scatter_fusion.1
  441.7 3.3 scatter_fusion.1
  447.5 3.3 scatter_fusion.1
  452.2 1.2 convolution_select_fusion.5
  453.4 3.3 scatter_fusion.1
  459.3 3.3 scatter_fusion.1
  465.1 3.3 scatter_fusion.1
  471.0 3.3 scatter_fusion.1
  476.9 3.3 scatter_fusion.1
  482.8 3.3 scatter_fusion.1
  488.6 3.3 scatter_fusion.1
  494.5 3.3 scatter_fusion.1
  500.4 3.3 scatter_fusion.1
  506.3 3.3 scatter_fusion.1
  512.1 3.3 scatter_fusion.1
  515.4 3.8 convert_element_type.29
  519.3 216.1 %reduce-scatter.5.cloned.1.call-done = bf16[128,256]{1,0:T(8,128)(2,1)} async-done(((bf16[4096,256]{1,0:T(8,128)(2,1)}), bf16[128,256]{1,0:T(8,128)(2,1)}) %reduce-scatter.5.cloned.1.call-update) | async-done | bytes 65552 | tf_op jit(solution)/shard_map/reduce_scatter | solution.py:45
  735.3 1.5 multiply_add_fusion
  (143 shorter events, 78.0 us)
Async XLA Ops:
  6.5 52.1 %copy-start.3 = (s32[1,1,128]{2,1,0:T(1,128)S(1)}, s32[1,1,128]{2,1,0:T(1,128)}, u32[]{:S(2)}) copy-start(s32[1,1,128]{2,1,0:T(1,128)} %param.11) | copy-start | bytes 1540
  6.5 52.1 %copy-start.4 = (s32[1,1,128]{2,1,0:T(1,128)S(1)}, s32[1,1,128]{2,1,0:T(1,128)}, u32[]{:S(2)}) copy-start(s32[1,1,128]{2,1,0:T(1,128)} %param.12) | copy-start | bytes 1540
  6.5 49.7 %all-gather.3.cloned.1.call-start = ((), (), s32[]{:S(2)}) async-start(), calls=%async_computation.2 | async-start | bytes 1114112 | tf_op jit(solution)/shard_map/all_gather | solution.py:23
  8.1 364.2 %reduce-scatter.3.cloned.1.call-start = ((), (), s32[]{:S(2)}) async-start(), calls=%async_computation.3 | async-start | bytes 2162688 | tf_op jit(solution)/shard_map/reduce_scatter | solution.py:45
  56.2 2.4 copy-start.1
  152.6 219.7 %copy-start.2 = (f32[128,256]{1,0:T(8,128)S(1)}, f32[128,256]{1,0:T(8,128)}, u32[]{:S(2)}) copy-start(f32[128,256]{1,0:T(8,128)} %param.9) | copy-start | bytes 393220
  156.5 262.6 %all-gather.5.cloned.1.call-start = ((), (), s32[]{:S(2)}) async-start(), calls=%async_computation.4 | async-start | bytes 1114112 | tf_op jit(solution)/shard_map/all_gather | solution.py:23
  373.8 361.5 %reduce-scatter.5.cloned.1.call-start = ((), (), s32[]{:S(2)}) async-start(), calls=%async_computation.5 | async-start | bytes 2162688 | tf_op jit(solution)/shard_map/reduce_scatter | solution.py:45
  419.1 2.4 copy-start
Sparse Core Ops, SparseCore 0:
  9.5 46.6 all-gather.2
  156.6 215.6 reduce-scatter.2
  374.7 44.3 all-gather.4
  519.4 215.9 reduce-scatter.4
where the time goes:
time: 750 us; the launch traced here: 743 us
  waiting for transfers between devices  525 us (70%)
  other arithmetic  141 us (19%)
  matrix products  39.6 us (5%)
  local copies, waits for them, and re-layouts  23.5 us (3%)
  between operations  13.1 us (2%)
    reduce_scatter x2, waiting for transfers between devices, body(): lax.psum_scatter(partial_value.reshape(col_count * tile_size, classes).as...  432 us
    scatter-add x32, other arithmetic, advance(): return running.at[target].add(products)  106 us
    all_gather x2, waiting for transfers between devices, body(): lax.all_gather(current.astype(jnp.bfloat16), 'row', axis=0, tiled=True)  93.2 us
    dot_general x32, matrix products, advance(): jnp.einsum('gtk,gkc->gtc', block_tiles, sources, preferred_element_type=j...  39.6 us
    select_n x32, other arithmetic, advance(): return running.at[target].add(products)  23.1 us
    gather x32, local copies, waits for them, and re-layouts, advance(): sources = panels[source_cols]  18.6 us
  transfers between devices with their start and end apart: 4, of which 4 were waited for; matrix products, arithmetic and copies ran while one was open for 0% of the time, Pallas kernels for 0%

commit v1 on v0

v1 whole, which is shorter than its diff:
```python
import functools

import jax
import jax.numpy as jnp
from jax import lax
from jax.experimental import pallas as pl
from jax.experimental.pallas import tpu as pltpu
from jax.sharding import PartitionSpec as P

HOPS = 2
HALVES = 2
LANES = 128
WINDOW = 3
UNROLL = 32
MESH = pl.DeviceIdType.MESH


def spread(k, n):
    m = (k + 1) // 2
    return n // 2 + m * (1 - 2 * lax.rem(k, 2)) if not isinstance(k, int) else n // 2 + (-m if k % 2 else m)


def kernel(nx, ny, nz, *refs):
    (tiles_hbm, rows_s, cols_s, counts_s, logits, out, tv, prod, last,
     panel00, panel01, panel10, panel11, part, xrecv, zsend, zrecv, zown,
     tile_sem, ag_send, ag_recv, sib_send, sib_recv, x_send, x_recv, z_send, z_recv) = refs
    panel = ((panel00, panel01), (panel10, panel11))
    cap, tile = tv.shape[0], tv.shape[1]
    nrow, ncol = 2 * ny, nx * nz
    row, col = lax.axis_index("row"), lax.axis_index("col")
    x, z = col // nz, lax.rem(col, nz)
    sibling = (row + 1 - 2 * lax.rem(row, 2), col)

    def at_y(d):
        return (lax.rem(row + 2 * d, nrow), col)

    def at_x(d):
        return (row, lax.rem(col + nz * d, ncol))

    def at_z(d):
        return (row, x * nz + lax.rem(z + d, nz))

    load = pltpu.make_async_copy(tiles_hbm.at[0, 0], tv, tile_sem)
    load.start()
    for h in range(HALVES):
        panel[0][h][row] = logits[:, h * LANES:(h + 1) * LANES].astype(jnp.bfloat16)

    barrier = pltpu.get_barrier_semaphore()
    peers = [at_y(d) for d in range(1, ny)] + [at_x(d) for d in range(1, nx)] + [at_z(d) for d in range(1, nz)] + [sibling]
    for peer in peers:
        pl.semaphore_signal(barrier, inc=1, device_id=peer, device_id_type=MESH)
    pl.semaphore_wait(barrier, len(peers))

    def remote(src, dst, send_sem, recv_sem, device):
        return pltpu.make_async_remote_copy(src_ref=src, dst_ref=dst, send_sem=send_sem, recv_sem=recv_sem,
                                            device_id=device, device_id_type=MESH)

    def gather_start(t, h):
        p = panel[t][h]

        def step(k, carry):
            remote(p.at[row], p.at[row], ag_send.at[t, h], ag_recv.at[t, h, k], at_y(spread(k, ny))).start()
            return carry

        lax.fori_loop(0, ny - 1, step, 0)
        remote(p.at[row], p.at[row], sib_send.at[t, h], sib_recv.at[t, h], sibling).start()

    def gather_finish(t, h):
        p = panel[t][h]

        def step(k, carry):
            source = lax.rem(row + nrow - 2 * spread(k, ny), nrow)
            block = p.at[source]
            remote(block, block, ag_send.at[t, h], ag_recv.at[t, h, k], sibling).wait_recv()
            remote(block, block, sib_send.at[t, h], sib_recv.at[t, h], sibling).start()
            return carry

        lax.fori_loop(0, ny - 1, step, 0)
        most = p.at[pl.ds(0, ny)]
        remote(most, most, sib_send.at[t, h], sib_recv.at[t, h], sibling).wait_recv()

    def products(t, h):
        p = panel[t][h]
        unroll = min(UNROLL, cap)

        def group(g, total):
            terms = [
                jnp.dot(tv[g * unroll + u], p[cols_s[0, 0, g * unroll + u]], preferred_element_type=jnp.float32)
                for u in range(unroll)
            ]
            for u in range(unroll):
                s = g * unroll + u
                same = (rows_s[0, 0, s] == rows_s[0, 0, jnp.maximum(s - 1, 0)]).astype(jnp.float32)
                total = total * same + terms[u]
                prod[s] = total.astype(jnp.bfloat16)
            return total

        lax.fori_loop(0, cap // unroll, group, jnp.zeros((tile, LANES), jnp.float32))

        def place(r, carry):
            part[t, h, r] = prod[last[r]]
            return carry

        lax.fori_loop(0, ncol, place, 0, unroll=4)

    def x_start(t, h, k):
        block = lax.rem(z + spread(k, nz), nz)
        for e in (2, 1, 3) if nx == 4 else range(1, nx):
            target = lax.rem(x + e, nx) * nz + block
            remote(part.at[t, h, target], xrecv.at[t, h, k, e - 1], x_send.at[t, h], x_recv.at[t, h, k], at_x(e)).start()

    def x_sum(t, h, k):
        arrived = xrecv.at[t, h, k]
        remote(arrived, arrived, x_send.at[t, h], x_recv.at[t, h, k], sibling).wait_recv()
        total = part[t, h, x * nz + lax.rem(z + spread(k, nz), nz)].astype(jnp.float32)
        for e in range(nx - 1):
            total += xrecv[t, h, k, e].astype(jnp.float32)
        return total

    def x_step(t, h, k):
        zsend[t, h, k] = x_sum(t, h, k).astype(jnp.bfloat16)
        remote(zsend.at[t, h, k], zrecv.at[t, h, k], z_send.at[t, h], z_recv.at[t, h], at_z(spread(k, nz))).start()

    def x_run(t, h, lo, hi, follow):
        def step(k, carry):
            x_step(t, h, k)
            if follow is not None:
                x_start(follow[0], follow[1], k + follow[2])
            return carry

        lax.fori_loop(lo, hi, step, 0)

    def x_last(t, h):
        zown[t, h] = x_sum(t, h, nz - 1)

    def finish(t, h):
        arrived = zrecv.at[t, h]
        remote(arrived, arrived, z_send.at[t, h], z_recv.at[t, h], sibling).wait_recv()
        total = zown[t, h]
        for k in range(nz - 1):
            total += zrecv[t, h, k].astype(jnp.float32)
        lanes = slice(h * LANES, (h + 1) * LANES)
        current = 0.9 * total + 0.1 * logits[:, lanes]
        if t + 1 < HOPS:
            panel[t + 1][h][row] = current.astype(jnp.bfloat16)
        else:
            out[:, lanes] = current

    def sent(t, h):
        some = panel[t][h].at[pl.ds(0, ny - 1)]
        remote(some, some, ag_send.at[t, h], ag_recv.at[t, h, 0], sibling).wait_send()
        some = panel[t][h].at[pl.ds(0, ny)]
        remote(some, some, sib_send.at[t, h], sib_recv.at[t, h], sibling).wait_send()
        some = part.at[t, h, pl.ds(0, (nx - 1) * nz)]
        remote(some, some, x_send.at[t, h], x_recv.at[t, h, 0], sibling).wait_send()
        some = zsend.at[t, h]
        remote(some, some, z_send.at[t, h], z_recv.at[t, h], sibling).wait_send()

    window = min(WINDOW, nz - 1)

    def x_open(t, h):
        for k in range(window):
            x_start(t, h, k)

    gather_start(0, 0)
    gather_start(0, 1)

    prod[cap] = jnp.zeros((tile, LANES), jnp.bfloat16)
    count = counts_s[0, 0]

    def find(r, carry):
        place = jnp.int32(0)
        step = cap
        while step:
            tried = place + step
            fits = (tried <= count) & (rows_s[0, 0, jnp.minimum(tried, cap) - 1] <= r)
            place = jnp.where(fits, tried, place)
            step //= 2
        found = (place > 0) & (rows_s[0, 0, jnp.maximum(place - 1, 0)] == r)
        last[r] = jnp.where(found, place - 1, cap)
        return carry

    lax.fori_loop(0, ncol, find, 0)
    load.wait()

    gather_finish(0, 0)
    products(0, 0)
    x_open(0, 0)
    gather_finish(0, 1)
    products(0, 1)
    x_run(0, 0, 0, nz - window, (0, 0, window))
    x_run(0, 0, nz - window, nz - 1, (0, 1, window - nz))
    x_last(0, 0)
    x_start(0, 1, window - 1)
    early = min(3, nz - window)
    x_run(0, 1, 0, early, (0, 1, window))
    finish(0, 0)
    gather_start(1, 0)
    x_run(0, 1, early, nz - window, (0, 1, window))
    x_run(0, 1, nz - window, nz - 1, None)
    x_last(0, 1)
    gather_finish(1, 0)
    products(1, 0)
    x_open(1, 0)
    finish(0, 1)
    gather_start(1, 1)
    x_run(1, 0, 0, nz - window, (1, 0, window))
    x_run(1, 0, nz - window, nz - 1, None)
    x_last(1, 0)
    gather_finish(1, 1)
    products(1, 1)
    x_open(1, 1)
    sent(0, 0)
    sent(0, 1)
    finish(1, 0)
    x_run(1, 1, 0, nz - window, (1, 1, window))
    x_run(1, 1, nz - window, nz - 1, None)
    x_last(1, 1)
    sent(1, 0)
    finish(1, 1)
    sent(1, 1)


def solution(mesh):
    nrow, ncol = mesh.shape["row"], mesh.shape["col"]
    ny = nrow // 2
    nx = 4 if ncol == 32 else 2
    nz = ncol // nx

    def body(logits, tile_values, tile_rows, tile_cols, tile_counts):
        cap, tile = tile_values.shape[2], tile_values.shape[3]
        half = jnp.bfloat16
        dma = pltpu.SemaphoreType.DMA
        both = (HOPS, HALVES)
        return pl.pallas_call(
            functools.partial(kernel, nx, ny, nz),
            out_shape=jax.ShapeDtypeStruct(logits.shape, jnp.float32),
            in_specs=[
                pl.BlockSpec(memory_space=pl.ANY),
                pl.BlockSpec(memory_space=pltpu.SMEM),
                pl.BlockSpec(memory_space=pltpu.SMEM),
                pl.BlockSpec(memory_space=pltpu.SMEM),
                pl.BlockSpec(memory_space=pltpu.VMEM),
            ],
            out_specs=pl.BlockSpec(memory_space=pltpu.VMEM),
            scratch_shapes=[
                pltpu.VMEM((cap, tile, tile), half),
                pltpu.VMEM((cap + 1, tile, LANES), half),
                pltpu.SMEM((ncol,), jnp.int32),
                *[pltpu.VMEM((nrow, tile, LANES), half) for unused in range(HOPS * HALVES)],
                pltpu.VMEM((*both, ncol, tile, LANES), half),
                pltpu.VMEM((*both, nz, nx - 1, tile, LANES), half),
                pltpu.VMEM((*both, nz - 1, tile, LANES), half),
                pltpu.VMEM((*both, nz - 1, tile, LANES), half),
                pltpu.VMEM((*both, tile, LANES), jnp.float32),
                dma,
                dma(both),
                dma((*both, ny - 1)),
                dma(both),
                dma(both),
                dma(both),
                dma((*both, nz)),
                dma(both),
                dma(both),
            ],
            compiler_params=pltpu.CompilerParams(
                collective_id=0, has_side_effects=True, vmem_limit_bytes=58 * 2**20
            ),
            name="propagate",
        )(tile_values, tile_rows, tile_cols, tile_counts, logits)

    return jax.shard_map(
        body,
        mesh=mesh,
        in_specs=(
            P(("row", "col"), None),
            P("row", "col", None, None, None),
            P("row", "col", None),
            P("row", "col", None),
            P("row", "col"),
        ),
        out_specs=P(("row", "col"), None),
        check_vma=False,
    )
```

time: 750 us -> 91.9 us (0.12)
  waiting for transfers between devices: 525 us -> 0 us
  other arithmetic: 141 us -> 0 us
  Pallas kernels: 0 us -> 89.5 us
  matrix products: 39.6 us -> 0 us
  local copies, waits for them, and re-layouts: 23.5 us -> 1.57 us
  between operations: 13.1 us -> 0.66 us
    reduce_scatter x2 -> x0, waiting for transfers between devices: 432 us -> none  [body(): lax.psum_scatter(partial_value.reshape(col_count * tile_size, classes).as...]
    scatter-add x32 -> x0, other arithmetic: 106 us -> none  [advance(): return running.at[target].add(products)]
    all_gather x2 -> x0, waiting for transfers between devices: 93.2 us -> none  [body(): lax.all_gather(current.astype(jnp.bfloat16), 'row', axis=0, tiled=True)]
    pallas_call x0 -> x1, Pallas kernels: none -> 89.5 us  [body(): pl.pallas_call(functools.partial(kernel, nx, ny, nz), out_shape=jax.Shape...]
    dot_general x32 -> x0, matrix products: 39.6 us -> none  [advance(): jnp.einsum('gtk,gkc->gtc', block_tiles, sources, preferred_element_type=j...]
    select_n x32 -> x0, other arithmetic: 23.1 us -> none  [advance(): return running.at[target].add(products)]
    gather x32 -> x0, local copies, waits for them, and re-layouts: 18.6 us -> none  [advance(): sources = panels[source_cols]]
    convert_element_type x4 -> x0, other arithmetic: 10.7 us -> none  [the longest x2 7.64 us: body(): partial_value.reshape(col_count * tile_size, classes).astype(jnp.bfloat16)]
  transfers between devices with their start and end apart: 4 -> 0, of which waited for: 4 -> 0; matrix products, arithmetic and copies ran while one was open for 0% -> 0% of each run, Pallas kernels for 0% -> 0%
where the time goes in v1:
time: 91.9 us; the launch traced here: 91.7 us
  Pallas kernels  89.5 us (97%)
  local copies, waits for them, and re-layouts  1.57 us (2%)
    pallas_call x1, Pallas kernels, body(): pl.pallas_call(functools.partial(kernel, nx, ny, nz), out_shape=jax.Shape...  89.5 us

profile of v1, /device:TPU:1, one launch (start us, length us, event | category | flops | bytes accessed | tf_op | source)
XLA Modules:
  0.0 91.7 jit_solution(12603139561901578603)
XLA Ops:
  0.7 89.5 %propagate.1 = f32[128,256]{1,0:T(8,128)} custom-call(bf16[1,1,128,128,128]{4,3,2,1,0:T(8,128)(2,1)} %refs_0_.1, s32[1,1,128]{2,1,0:T(1,128)} %refs_1_.1, s32[1,1,128]{2,1,0:T(1,128)} %refs_2_.1, s32[1,1]{1,0:T(1,128)S(6)} %copy.7.refs_3_, f32[128,256]{1,0:T(8,128)} %refs_4_.1), custom_call_target="tpu_custom_call" | custom-call | tf_op jit(solution)/shard_map/propagate/pallas_call | solution.py:235
  90.1 1.6 %copy.8 = f32[128,256]{1,0:T(8,128)} copy(f32[128,256]{1,0:T(8,128)} %propagate.1) | data formatting | bytes 262144

commit v2 on v1

v2 whole, which is shorter than its diff:
```python
import functools

import jax
import jax.numpy as jnp
from jax import lax
from jax.experimental import pallas as pl
from jax.experimental.pallas import tpu as pltpu
from jax.sharding import PartitionSpec as P

HOPS = 2
HALVES = 2
LANES = 128
UNROLL = 64
ROWS = 80
MESH = pl.DeviceIdType.MESH


def spread(k, n):
    m = (k + 1) // 2
    return n // 2 + m * (1 - 2 * lax.rem(k, 2)) if not isinstance(k, int) else n // 2 + (-m if k % 2 else m)


def kernel(nx, ny, nz, *refs):
    (tiles_hbm, rows_hbm, cols_hbm, counts_s, logits_hbm, out, tv, prod, last, rows_s, cols_s, logits,
     panel00, panel01, panel10, panel11, part, xrecv, zsend, zrecv, zown, zfrecv, zfmid, xfsend, xfrecv,
     in_sems, ag_send, ag_recv, sib_send, sib_recv, x_send, x_recv, z_send, z_recv,
     zf_send, zf_recv, xf_send, xf_recv) = refs
    panel = ((panel00, panel01), (panel10, panel11))
    cap, tile = tv.shape[0], tv.shape[1]
    nrow, ncol = 2 * ny, nx * nz
    row, col = lax.axis_index("row"), lax.axis_index("col")
    x, z, core = col // nz, lax.rem(col, nz), lax.rem(row, 2)
    sibling = (row + 1 - 2 * core, col)
    turn = 1 - 2 * core
    upper, lower = pl.ds(0, ROWS), pl.ds(ROWS, tile - ROWS)

    def at_y(d):
        return (lax.rem(row + 2 * (d + ny), nrow), col)

    def at_x(d):
        return (row, lax.rem(col + nz * d, ncol))

    def at_z(d):
        return (row, x * nz + lax.rem(z + d + nz, nz))

    barrier = pltpu.get_barrier_semaphore()
    ways = (1, -1, 2, -2)
    peers = [at_y(d) for d in ways] + [at_x(d) for d in range(1, nx)] + [at_z(d) for d in range(1, nz)] + [sibling]
    for peer in peers:
        pl.semaphore_signal(barrier, inc=1, device_id=peer, device_id_type=MESH)
    loads = [
        pltpu.make_async_copy(logits_hbm, logits, in_sems.at[0]),
        pltpu.make_async_copy(rows_hbm, rows_s, in_sems.at[1]),
        pltpu.make_async_copy(cols_hbm, cols_s, in_sems.at[2]),
        pltpu.make_async_copy(tiles_hbm.at[0, 0], tv, in_sems.at[3]),
    ]
    for load in loads:
        load.start()
    loads[0].wait()
    for h in range(HALVES):
        panel[0][h][row] = logits[:, h * LANES:(h + 1) * LANES].astype(jnp.bfloat16)
    pl.semaphore_wait(barrier, len(peers))

    def remote(src, dst, send_sem, recv_sem, device):
        return pltpu.make_async_remote_copy(src_ref=src, dst_ref=dst, send_sem=send_sem, recv_sem=recv_sem,
                                            device_id=device, device_id_type=MESH)

    def gather_send(t, h, block, slot, d):
        p = panel[t][h]
        remote(p.at[block], p.at[block], ag_send.at[t, h], ag_recv.at[t, h, slot], at_y(d)).start()

    def gather_start(t, h):
        p = panel[t][h]
        for slot, d in enumerate((2, -2, 1, -1)):
            gather_send(t, h, row, slot, d)
        remote(p.at[row], p.at[row], sib_send.at[t, h], sib_recv.at[t, h], sibling).start()

    def gather_wait(t, h, slot, d):
        p = panel[t][h]
        source = lax.rem(row + nrow - 2 * d, nrow)
        block = p.at[source]
        remote(block, block, ag_send.at[t, h], ag_recv.at[t, h, slot], sibling).wait_recv()
        remote(block, block, sib_send.at[t, h], sib_recv.at[t, h], sibling).start()
        return source

    def gather_mid(t, h):
        first = []
        for slot, d in enumerate((2, -2)):
            p = panel[t][h]
            source = lax.rem(row + nrow - 2 * d, nrow)
            block = p.at[source]
            remote(block, block, ag_send.at[t, h], ag_recv.at[t, h, slot], sibling).wait_recv()
            gather_send(t, h, source, 4 + slot, d // 2)
            first.append(source)
        gather_send(t, h, lax.rem(row + nrow - 4 * turn, nrow), 6, 2 * turn)
        for source in first:
            block = panel[t][h].at[source]
            remote(block, block, sib_send.at[t, h], sib_recv.at[t, h], sibling).start()

    def gather_finish(t, h):
        for slot, d in ((2, 1), (3, -1), (4, 3), (5, -3), (6, 4)):
            gather_wait(t, h, slot, d)
        most = panel[t][h].at[pl.ds(0, ny)]
        remote(most, most, sib_send.at[t, h], sib_recv.at[t, h], sibling).wait_recv()

    def products(t, h):
        p = panel[t][h]
        unroll = min(UNROLL, cap)

        def group(g, total):
            terms = [
                jnp.dot(tv[g * unroll + u], p[cols_s[0, 0, g * unroll + u]], preferred_element_type=jnp.float32)
                for u in range(unroll)
            ]
            for u in range(unroll):
                s = g * unroll + u
                same = (rows_s[0, 0, s] == rows_s[0, 0, jnp.maximum(s - 1, 0)]).astype(jnp.float32)
                total = total * same + terms[u]
                prod[s] = total.astype(jnp.bfloat16)
            return total

        lax.fori_loop(0, cap // unroll, group, jnp.zeros((tile, LANES), jnp.float32))

        def place(r, carry):
            part[t, h, r // nz, lax.rem(r, nz)] = prod[last[r]]
            return carry

        lax.fori_loop(0, ncol, place, 0, unroll=4)

    def x_start(t, h, k):
        block = lax.rem(z + spread(k, nz), nz)
        for e in (2, 1, 3):
            target = lax.rem(x + e, nx)
            remote(part.at[t, h, target, block, upper], xrecv.at[t, h, k, e - 1], x_send.at[t, h], x_recv.at[t, h, k], at_x(e)).start()

    def x_sum(t, h, k):
        arrived = xrecv.at[t, h, k]
        remote(arrived, arrived, x_send.at[t, h], x_recv.at[t, h, k], sibling).wait_recv()
        total = part[t, h, x, lax.rem(z + spread(k, nz), nz), upper].astype(jnp.float32)
        for e in range(nx - 1):
            total += xrecv[t, h, k, e].astype(jnp.float32)
        return total

    def x_step(t, h, k):
        zsend[t, h, k] = x_sum(t, h, k).astype(jnp.bfloat16)
        remote(zsend.at[t, h, k], zrecv.at[t, h, k], z_send.at[t, h], z_recv.at[t, h], at_z(spread(k, nz))).start()

    def x_run(t, h, lo, hi):
        def step(k, carry):
            x_step(t, h, k)
            return carry

        lax.fori_loop(lo, hi, step, 0)

    def x_last(t, h):
        zown[t, h] = x_sum(t, h, nz - 1)

    def zf_block(t, h, d):
        return part.at[t, h, :, lax.rem(z + d + nz, nz), lower]

    def zf_send_to(t, h, source, slot, sem, d):
        remote(source, zfrecv.at[t, h, slot], zf_send.at[t, h], zf_recv.at[t, h, sem], at_z(d)).start()

    def zf_start(t, h):
        zf_send_to(t, h, zf_block(t, h, 4 * turn), 0, 0, 2 * turn)
        zf_send_to(t, h, zf_block(t, h, 3 * turn), 1, 0, turn)
        zf_send_to(t, h, zf_block(t, h, -3 * turn), 2, 1, -turn)
        zf_send_to(t, h, zf_block(t, h, turn), 3, 2, turn)
        zf_send_to(t, h, zf_block(t, h, -turn), 4, 2, -turn)

    def zf_wait(t, h, lo, n, sem):
        arrived = zfrecv.at[t, h, pl.ds(lo, n)]
        remote(arrived, arrived, zf_send.at[t, h], zf_recv.at[t, h, sem], sibling).wait_recv()

    def zf_own(t, h, d):
        return part[t, h, :, lax.rem(z + d + nz, nz), lower].astype(jnp.float32)

    def zf_mid(t, h):
        zf_wait(t, h, 0, 2, 0)
        total = zf_own(t, h, 2 * turn) + zfrecv[t, h, 0].astype(jnp.float32) + zfrecv[t, h, 1].astype(jnp.float32)
        zfmid[t, h, 0] = total.astype(jnp.bfloat16)
        zf_send_to(t, h, zfmid.at[t, h, 0], 5, 2, 2 * turn)
        zf_wait(t, h, 2, 1, 1)
        total = zf_own(t, h, -2 * turn) + zfrecv[t, h, 2].astype(jnp.float32)
        zfmid[t, h, 1] = total.astype(jnp.bfloat16)
        zf_send_to(t, h, zfmid.at[t, h, 1], 6, 2, -2 * turn)

    def zf_end(t, h):
        zf_wait(t, h, 3, 4, 2)
        total = zf_own(t, h, 0)
        for slot in range(3, 7):
            total += zfrecv[t, h, slot].astype(jnp.float32)
        xfsend[t, h] = total.astype(jnp.bfloat16)
        for e in (2, 1, 3):
            remote(xfsend.at[t, h, lax.rem(x + e, nx)], xfrecv.at[t, h, e - 1], xf_send.at[t, h], xf_recv.at[t, h], at_x(e)).start()

    def finish(t, h):
        arrived = zrecv.at[t, h]
        remote(arrived, arrived, z_send.at[t, h], z_recv.at[t, h], sibling).wait_recv()
        total = zown[t, h]
        for k in range(nz - 1):
            total += zrecv[t, h, k].astype(jnp.float32)
        lanes = slice(h * LANES, (h + 1) * LANES)

        def store(part_rows, total):
            current = 0.9 * total + 0.1 * logits[part_rows, lanes]
            if t + 1 < HOPS:
                panel[t + 1][h][row, part_rows] = current.astype(jnp.bfloat16)
            else:
                out[part_rows, lanes] = current

        store(slice(0, ROWS), total)
        arrived = xfrecv.at[t, h]
        remote(arrived, arrived, xf_send.at[t, h], xf_recv.at[t, h], sibling).wait_recv()
        total = xfsend[t, h, x].astype(jnp.float32)
        for e in range(nx - 1):
            total += xfrecv[t, h, e].astype(jnp.float32)
        store(slice(ROWS, tile), total)

    def sent(t, h):
        some = panel[t][h].at[pl.ds(0, ny - 1)]
        remote(some, some, ag_send.at[t, h], ag_recv.at[t, h, 0], sibling).wait_send()
        some = panel[t][h].at[pl.ds(0, ny)]
        remote(some, some, sib_send.at[t, h], sib_recv.at[t, h], sibling).wait_send()
        some = xrecv.at[t, h]
        remote(some, some, x_send.at[t, h], x_recv.at[t, h, 0], sibling).wait_send()
        some = zsend.at[t, h]
        remote(some, some, z_send.at[t, h], z_recv.at[t, h], sibling).wait_send()
        some = zfrecv.at[t, h]
        remote(some, some, zf_send.at[t, h], zf_recv.at[t, h, 0], sibling).wait_send()
        some = xfrecv.at[t, h]
        remote(some, some, xf_send.at[t, h], xf_recv.at[t, h], sibling).wait_send()

    def open_all(t, h):
        def step(k, carry):
            x_start(t, h, k)
            return carry

        zf_start(t, h)
        lax.fori_loop(0, nz, step, 0)

    gather_start(0, 0)

    prod[cap] = jnp.zeros((tile, LANES), jnp.bfloat16)
    count = counts_s[0, 0]

    def find(r, carry):
        place = jnp.int32(0)
        step = cap
        while step:
            tried = place + step
            fits = (tried <= count) & (rows_s[0, 0, jnp.minimum(tried, cap) - 1] <= r)
            place = jnp.where(fits, tried, place)
            step //= 2
        found = (place > 0) & (rows_s[0, 0, jnp.maximum(place - 1, 0)] == r)
        last[r] = jnp.where(found, place - 1, cap)
        return carry

    loads[1].wait()
    loads[2].wait()
    lax.fori_loop(0, ncol // 2, find, 0)
    gather_mid(0, 0)
    gather_start(0, 1)
    lax.fori_loop(ncol // 2, ncol, find, 0)
    loads[3].wait()

    gather_finish(0, 0)
    products(0, 0)
    open_all(0, 0)
    gather_mid(0, 1)
    x_run(0, 0, 0, 2)
    zf_mid(0, 0)
    gather_finish(0, 1)
    products(0, 1)
    open_all(0, 1)
    x_run(0, 0, 2, nz - 1)
    x_last(0, 0)
    zf_end(0, 0)
    x_run(0, 1, 0, 2)
    zf_mid(0, 1)
    finish(0, 0)
    gather_start(1, 0)
    x_run(0, 1, 2, nz - 1)
    x_last(0, 1)
    zf_end(0, 1)
    gather_mid(1, 0)
    finish(0, 1)
    gather_start(1, 1)
    gather_finish(1, 0)
    products(1, 0)
    open_all(1, 0)
    gather_mid(1, 1)
    x_run(1, 0, 0, 2)
    zf_mid(1, 0)
    gather_finish(1, 1)
    products(1, 1)
    open_all(1, 1)
    sent(0, 0)
    sent(0, 1)
    x_run(1, 0, 2, nz - 1)
    x_last(1, 0)
    zf_end(1, 0)
    x_run(1, 1, 0, 2)
    zf_mid(1, 1)
    finish(1, 0)
    x_run(1, 1, 2, nz - 1)
    x_last(1, 1)
    zf_end(1, 1)
    sent(1, 0)
    finish(1, 1)
    sent(1, 1)


def solution(mesh):
    nrow, ncol = mesh.shape["row"], mesh.shape["col"]
    ny = nrow // 2
    nx = 4 if ncol == 32 else 2
    nz = ncol // nx

    def body(logits, tile_values, tile_rows, tile_cols, tile_counts):
        cap, tile = tile_values.shape[2], tile_values.shape[3]
        half = jnp.bfloat16
        dma = pltpu.SemaphoreType.DMA
        both = (HOPS, HALVES)
        return pl.pallas_call(
            functools.partial(kernel, nx, ny, nz),
            out_shape=jax.ShapeDtypeStruct(logits.shape, jnp.float32),
            in_specs=[
                pl.BlockSpec(memory_space=pl.ANY),
                pl.BlockSpec(memory_space=pl.ANY),
                pl.BlockSpec(memory_space=pl.ANY),
                pl.BlockSpec(memory_space=pltpu.SMEM),
                pl.BlockSpec(memory_space=pl.ANY),
            ],
            out_specs=pl.BlockSpec(memory_space=pltpu.VMEM),
            scratch_shapes=[
                pltpu.VMEM((cap, tile, tile), half),
                pltpu.VMEM((cap + 1, tile, LANES), half),
                pltpu.SMEM((ncol,), jnp.int32),
                pltpu.SMEM((1, 1, cap), jnp.int32),
                pltpu.SMEM((1, 1, cap), jnp.int32),
                pltpu.VMEM(logits.shape, jnp.float32),
                *[pltpu.VMEM((nrow, tile, LANES), half) for unused in range(HOPS * HALVES)],
                pltpu.VMEM((*both, nx, nz, tile, LANES), half),
                pltpu.VMEM((*both, nz, nx - 1, ROWS, LANES), half),
                pltpu.VMEM((*both, nz - 1, ROWS, LANES), half),
                pltpu.VMEM((*both, nz - 1, ROWS, LANES), half),
                pltpu.VMEM((*both, ROWS, LANES), jnp.float32),
                pltpu.VMEM((*both, 7, nx, tile - ROWS, LANES), half),
                pltpu.VMEM((*both, 2, nx, tile - ROWS, LANES), half),
                pltpu.VMEM((*both, nx, tile - ROWS, LANES), half),
                pltpu.VMEM((*both, nx - 1, tile - ROWS, LANES), half),
                dma((4,)),
                dma(both),
                dma((*both, 7)),
                dma(both),
                dma(both),
                dma(both),
                dma((*both, nz)),
                dma(both),
                dma(both),
                dma(both),
                dma((*both, 3)),
                dma(both),
                dma(both),
            ],
            compiler_params=pltpu.CompilerParams(
                collective_id=0, has_side_effects=True, vmem_limit_bytes=58 * 2**20
            ),
            name="propagate",
        )(tile_values, tile_rows, tile_cols, tile_counts, logits)

    return jax.shard_map(
        body,
        mesh=mesh,
        in_specs=(
            P(("row", "col"), None),
            P("row", "col", None, None, None),
            P("row", "col", None),
            P("row", "col", None),
            P("row", "col"),
        ),
        out_specs=P(("row", "col"), None),
        check_vma=False,
    )
```

time: 91.9 us -> 81.7 us (0.89)
  Pallas kernels: 89.5 us -> 79.4 us
    pallas_call x1, Pallas kernels: 89.5 us -> 79.4 us  [body(): pl.pallas_call(functools.partial(kernel, nx, ny, nz), out_shape=jax.Shape...]
where the time goes in v2:
time: 81.7 us; the launch traced here: 81.6 us
  Pallas kernels  79.4 us (97%)
  local copies, waits for them, and re-layouts  1.57 us (2%)
    pallas_call x1, Pallas kernels, body(): pl.pallas_call(functools.partial(kernel, nx, ny, nz), out_shape=jax.Shape...  79.4 us

profile of v2, /device:TPU:1, one launch (start us, length us, event | category | flops | bytes accessed | tf_op | source)
XLA Modules:
  0.0 81.6 jit_solution(6574466966959036678)
XLA Ops:
  0.7 79.4 %propagate.1 = f32[128,256]{1,0:T(8,128)} custom-call(bf16[1,1,128,128,128]{4,3,2,1,0:T(8,128)(2,1)} %refs_0_.1, s32[1,1,128]{2,1,0:T(1,128)} %refs_1_.1, s32[1,1,128]{2,1,0:T(1,128)} %refs_2_.1, s32[1,1]{1,0:T(1,128)S(6)} %copy.7.refs_3_, f32[128,256]{1,0:T(8,128)} %refs_4_.1), custom_call_target="tpu_custom_call" | custom-call | tf_op jit(solution)/shard_map/propagate/pallas_call | solution.py:325
  80.0 1.6 %copy.8 = f32[128,256]{1,0:T(8,128)} copy(f32[128,256]{1,0:T(8,128)} %propagate.1) | data formatting | bytes 262144

commit v3 on v2

--- a/solution.py
+++ b/solution.py
@@ -12,6 +12,7 @@
 LANES = 128
 UNROLL = 64
 ROWS = 80
+BOUNDS = (0, 2, 4, 6, 8)
 MESH = pl.DeviceIdType.MESH
 
 
@@ -121,73 +122,74 @@
 
         lax.fori_loop(0, cap // unroll, group, jnp.zeros((tile, LANES), jnp.float32))
 
-        def place(r, carry):
-            part[t, h, r // nz, lax.rem(r, nz)] = prod[last[r]]
+        def place(k, carry):
+            block = lax.rem(z + spread(k, nz), nz)
+            for target in range(nx):
+                part[t, h, target, k] = prod[last[target * nz + block]]
             return carry
 
-        lax.fori_loop(0, ncol, place, 0, unroll=4)
-
-    def x_start(t, h, k):
-        block = lax.rem(z + spread(k, nz), nz)
+        lax.fori_loop(0, nz, place, 0)
+
+    def x_start(t, h, g):
+        some = pl.ds(BOUNDS[g], BOUNDS[g + 1] - BOUNDS[g])
         for e in (2, 1, 3):
             target = lax.rem(x + e, nx)
-            remote(part.at[t, h, target, block, upper], xrecv.at[t, h, k, e - 1], x_send.at[t, h], x_recv.at[t, h, k], at_x(e)).start()
+            remote(part.at[t, h, target, some, upper], xrecv.at[t, h, e - 1, some], x_send.at[t, h], x_recv.at[t, h, g], at_x(e)).start()
 
     def x_sum(t, h, k):
-        arrived = xrecv.at[t, h, k]
-        remote(arrived, arrived, x_send.at[t, h], x_recv.at[t, h, k], sibling).wait_recv()
-        total = part[t, h, x, lax.rem(z + spread(k, nz), nz), upper].astype(jnp.float32)
+        total = part[t, h, x, k, upper].astype(jnp.float32)
         for e in range(nx - 1):
-            total += xrecv[t, h, k, e].astype(jnp.float32)
+            total += xrecv[t, h, e, k].astype(jnp.float32)
         return total
 
-    def x_step(t, h, k):
-        zsend[t, h, k] = x_sum(t, h, k).astype(jnp.bfloat16)
-        remote(zsend.at[t, h, k], zrecv.at[t, h, k], z_send.at[t, h], z_recv.at[t, h], at_z(spread(k, nz))).start()
-
-    def x_run(t, h, lo, hi):
-        def step(k, carry):
-            x_step(t, h, k)
-            return carry
-
-        lax.fori_loop(lo, hi, step, 0)
-
-    def x_last(t, h):
-        zown[t, h] = x_sum(t, h, nz - 1)
-
-    def zf_block(t, h, d):
-        return part.at[t, h, :, lax.rem(z + d + nz, nz), lower]
+    def x_run(t, h, first, past):
+        for g in range(first, past):
+            lo, hi = BOUNDS[g], BOUNDS[g + 1]
+            arrived = xrecv.at[t, h, :, pl.ds(lo, hi - lo)]
+            remote(arrived, arrived, x_send.at[t, h], x_recv.at[t, h, g], sibling).wait_recv()
+
+            def step(k, carry):
+                zsend[t, h, k] = x_sum(t, h, k).astype(jnp.bfloat16)
+                remote(zsend.at[t, h, k], zrecv.at[t, h, k], z_send.at[t, h], z_recv.at[t, h], at_z(spread(k, nz))).start()
+                return carry
+
+            lax.fori_loop(lo, min(hi, nz - 1), step, 0)
+        if past == len(BOUNDS) - 1:
+            zown[t, h] = x_sum(t, h, nz - 1)
+
+    def zf_block(t, h, k):
+        return part.at[t, h, :, k, lower]
 
     def zf_send_to(t, h, source, slot, sem, d):
         remote(source, zfrecv.at[t, h, slot], zf_send.at[t, h], zf_recv.at[t, h, sem], at_z(d)).start()
 
     def zf_start(t, h):
-        zf_send_to(t, h, zf_block(t, h, 4 * turn), 0, 0, 2 * turn)
-        zf_send_to(t, h, zf_block(t, h, 3 * turn), 1, 0, turn)
-        zf_send_to(t, h, zf_block(t, h, -3 * turn), 2, 1, -turn)
-        zf_send_to(t, h, zf_block(t, h, turn), 3, 2, turn)
-        zf_send_to(t, h, zf_block(t, h, -turn), 4, 2, -turn)
+        zf_send_to(t, h, zf_block(t, h, 0), 0, 0, 2 * turn)
+        zf_send_to(t, h, zf_block(t, h, 1 + core), 1, 0, turn)
+        zf_send_to(t, h, zf_block(t, h, 2 - core), 2, 1, -turn)
+        zf_send_to(t, h, zf_block(t, h, 5 + core), 3, 2, turn)
+        zf_send_to(t, h, zf_block(t, h, 6 - core), 4, 2, -turn)
 
     def zf_wait(t, h, lo, n, sem):
         arrived = zfrecv.at[t, h, pl.ds(lo, n)]
         remote(arrived, arrived, zf_send.at[t, h], zf_recv.at[t, h, sem], sibling).wait_recv()
 
-    def zf_own(t, h, d):
-        return part[t, h, :, lax.rem(z + d + nz, nz), lower].astype(jnp.float32)
+    def zf_own(t, h, k):
+        return part[t, h, :, k, lower].astype(jnp.float32)
 
     def zf_mid(t, h):
         zf_wait(t, h, 0, 2, 0)
-        total = zf_own(t, h, 2 * turn) + zfrecv[t, h, 0].astype(jnp.float32) + zfrecv[t, h, 1].astype(jnp.float32)
+        total = zf_own(t, h, 3 + core) + zfrecv[t, h, 0].astype(jnp.float32) + zfrecv[t, h, 1].astype(jnp.float32)
         zfmid[t, h, 0] = total.astype(jnp.bfloat16)
         zf_send_to(t, h, zfmid.at[t, h, 0], 5, 2, 2 * turn)
         zf_wait(t, h, 2, 1, 1)
-        total = zf_own(t, h, -2 * turn) + zfrecv[t, h, 2].astype(jnp.float32)
+        total = zf_own(t, h, 4 - core) + zfrecv[t, h, 2].astype(jnp.float32)
         zfmid[t, h, 1] = total.astype(jnp.bfloat16)
         zf_send_to(t, h, zfmid.at[t, h, 1], 6, 2, -2 * turn)
 
     def zf_end(t, h):
         zf_wait(t, h, 3, 4, 2)
-        total = zf_own(t, h, 0)
+        total = zf_own(t, h, nz - 1)
         for slot in range(3, 7):
             total += zfrecv[t, h, slot].astype(jnp.float32)
         xfsend[t, h] = total.astype(jnp.bfloat16)
@@ -231,13 +233,12 @@
         some = xfrecv.at[t, h]
         remote(some, some, xf_send.at[t, h], xf_recv.at[t, h], sibling).wait_send()
 
+    groups = len(BOUNDS) - 1
+
     def open_all(t, h):
-        def step(k, carry):
-            x_start(t, h, k)
-            return carry
-
         zf_start(t, h)
-        lax.fori_loop(0, nz, step, 0)
+        for g in range(groups):
+            x_start(t, h, g)
 
     gather_start(0, 0)
 
@@ -268,20 +269,18 @@
     products(0, 0)
     open_all(0, 0)
     gather_mid(0, 1)
-    x_run(0, 0, 0, 2)
+    x_run(0, 0, 0, 1)
     zf_mid(0, 0)
     gather_finish(0, 1)
     products(0, 1)
     open_all(0, 1)
-    x_run(0, 0, 2, nz - 1)
-    x_last(0, 0)
+    x_run(0, 0, 1, groups)
     zf_end(0, 0)
-    x_run(0, 1, 0, 2)
+    x_run(0, 1, 0, 1)
     zf_mid(0, 1)
     finish(0, 0)
     gather_start(1, 0)
-    x_run(0, 1, 2, nz - 1)
-    x_last(0, 1)
+    x_run(0, 1, 1, groups)
     zf_end(0, 1)
     gather_mid(1, 0)
     finish(0, 1)
@@ -290,21 +289,19 @@
     products(1, 0)
     open_all(1, 0)
     gather_mid(1, 1)
-    x_run(1, 0, 0, 2)
+    x_run(1, 0, 0, 1)
     zf_mid(1, 0)
     gather_finish(1, 1)
     products(1, 1)
     open_all(1, 1)
     sent(0, 0)
     sent(0, 1)
-    x_run(1, 0, 2, nz - 1)
-    x_last(1, 0)
+    x_run(1, 0, 1, groups)
     zf_end(1, 0)
-    x_run(1, 1, 0, 2)
+    x_run(1, 1, 0, 1)
     zf_mid(1, 1)
     finish(1, 0)
-    x_run(1, 1, 2, nz - 1)
-    x_last(1, 1)
+    x_run(1, 1, 1, groups)
     zf_end(1, 1)
     sent(1, 0)
     finish(1, 1)
@@ -342,7 +339,7 @@
                 pltpu.VMEM(logits.shape, jnp.float32),
                 *[pltpu.VMEM((nrow, tile, LANES), half) for unused in range(HOPS * HALVES)],
                 pltpu.VMEM((*both, nx, nz, tile, LANES), half),
-                pltpu.VMEM((*both, nz, nx - 1, ROWS, LANES), half),
+                pltpu.VMEM((*both, nx - 1, nz, ROWS, LANES), half),
                 pltpu.VMEM((*both, nz - 1, ROWS, LANES), half),
                 pltpu.VMEM((*both, nz - 1, ROWS, LANES), half),
                 pltpu.VMEM((*both, ROWS, LANES), jnp.float32),

time: 81.7 us -> 80.6 us (0.987)
  Pallas kernels: 79.4 us -> 78.2 us
    pallas_call x1, Pallas kernels: 79.4 us -> 78.2 us  [body(): pl.pallas_call(functools.partial(kernel, nx, ny, nz), out_shape=jax.Shape...]
where the time goes in v3:
time: 80.6 us; the launch traced here: 80.4 us
  Pallas kernels  78.2 us (97%)
  local copies, waits for them, and re-layouts  1.57 us (2%)
    pallas_call x1, Pallas kernels, body(): pl.pallas_call(functools.partial(kernel, nx, ny, nz), out_shape=jax.Shape...  78.2 us

profile of v3, /device:TPU:1, one launch (start us, length us, event | category | flops | bytes accessed | tf_op | source)
XLA Modules:
  0.0 80.4 jit_solution(6013305209154298399)
XLA Ops:
  0.7 78.2 %propagate.1 = f32[128,256]{1,0:T(8,128)} custom-call(bf16[1,1,128,128,128]{4,3,2,1,0:T(8,128)(2,1)} %refs_0_.1, s32[1,1,128]{2,1,0:T(1,128)} %refs_1_.1, s32[1,1,128]{2,1,0:T(1,128)} %refs_2_.1, s32[1,1]{1,0:T(1,128)S(6)} %copy.7.refs_3_, f32[128,256]{1,0:T(8,128)} %refs_4_.1), custom_call_target="tpu_custom_call" | custom-call | tf_op jit(solution)/shard_map/propagate/pallas_call | solution.py:322
  78.9 1.6 %copy.8 = f32[128,256]{1,0:T(8,128)} copy(f32[128,256]{1,0:T(8,128)} %propagate.1) | data formatting | bytes 262144

commit v4 on v3

--- a/solution.py
+++ b/solution.py
@@ -10,15 +10,13 @@
 HOPS = 2
 HALVES = 2
 LANES = 128
-UNROLL = 64
+UNROLL = 128
 ROWS = 80
-BOUNDS = (0, 2, 4, 6, 8)
+BOUNDS = (0, 3, 6, 8)
+OFFSETS = (4, 3, -3, 1, -1, 0, 2, -2)
+STEPS = (2, 1, -1, 1, -1, 0, 2, -2)
+OWN = 5
 MESH = pl.DeviceIdType.MESH
-
-
-def spread(k, n):
-    m = (k + 1) // 2
-    return n // 2 + m * (1 - 2 * lax.rem(k, 2)) if not isinstance(k, int) else n // 2 + (-m if k % 2 else m)
 
 
 def kernel(nx, ny, nz, *refs):
@@ -46,7 +44,7 @@
 
     barrier = pltpu.get_barrier_semaphore()
     ways = (1, -1, 2, -2)
-    peers = [at_y(d) for d in ways] + [at_x(d) for d in range(1, nx)] + [at_z(d) for d in range(1, nz)] + [sibling]
+    peers = [at_y(d) for d in ways] + [at_x(d) for d in range(1, nx)] + [at_z(d) for d in ways] + [sibling]
     for peer in peers:
         pl.semaphore_signal(barrier, inc=1, device_id=peer, device_id_type=MESH)
     loads = [
@@ -122,13 +120,10 @@
 
         lax.fori_loop(0, cap // unroll, group, jnp.zeros((tile, LANES), jnp.float32))
 
-        def place(k, carry):
-            block = lax.rem(z + spread(k, nz), nz)
+        for k, d in enumerate(OFFSETS):
+            block = lax.rem(z + d * turn + nz, nz)
             for target in range(nx):
                 part[t, h, target, k] = prod[last[target * nz + block]]
-            return carry
-
-        lax.fori_loop(0, nz, place, 0)
 
     def x_start(t, h, g):
         some = pl.ds(BOUNDS[g], BOUNDS[g + 1] - BOUNDS[g])
@@ -142,20 +137,30 @@
             total += xrecv[t, h, e, k].astype(jnp.float32)
         return total
 
+    def z_wait(t, h, lo, n, sem):
+        arrived = zrecv.at[t, h, pl.ds(lo, n)]
+        remote(arrived, arrived, z_send.at[t, h], z_recv.at[t, h, sem], sibling).wait_recv()
+
     def x_run(t, h, first, past):
         for g in range(first, past):
             lo, hi = BOUNDS[g], BOUNDS[g + 1]
             arrived = xrecv.at[t, h, :, pl.ds(lo, hi - lo)]
             remote(arrived, arrived, x_send.at[t, h], x_recv.at[t, h, g], sibling).wait_recv()
-
-            def step(k, carry):
-                zsend[t, h, k] = x_sum(t, h, k).astype(jnp.bfloat16)
-                remote(zsend.at[t, h, k], zrecv.at[t, h, k], z_send.at[t, h], z_recv.at[t, h], at_z(spread(k, nz))).start()
-                return carry
-
-            lax.fori_loop(lo, min(hi, nz - 1), step, 0)
-        if past == len(BOUNDS) - 1:
-            zown[t, h] = x_sum(t, h, nz - 1)
+            for k in range(lo, hi):
+                total = x_sum(t, h, k)
+                if k == OWN:
+                    zown[t, h] = total
+                    continue
+                slot, sem = (k, (0, 0, 1, 2, 2)[k]) if k < OWN else (k - 1, 2)
+                if k == 6:
+                    z_wait(t, h, 0, 2, 0)
+                    total += zrecv[t, h, 0].astype(jnp.float32) + zrecv[t, h, 1].astype(jnp.float32)
+                if k == 7:
+                    z_wait(t, h, 2, 1, 1)
+                    total += zrecv[t, h, 2].astype(jnp.float32)
+                zsend[t, h, slot] = total.astype(jnp.bfloat16)
+                remote(zsend.at[t, h, slot], zrecv.at[t, h, slot], z_send.at[t, h], z_recv.at[t, h, sem],
+                       at_z(STEPS[k] * turn)).start()
 
     def zf_block(t, h, k):
         return part.at[t, h, :, k, lower]
@@ -165,10 +170,10 @@
 
     def zf_start(t, h):
         zf_send_to(t, h, zf_block(t, h, 0), 0, 0, 2 * turn)
-        zf_send_to(t, h, zf_block(t, h, 1 + core), 1, 0, turn)
-        zf_send_to(t, h, zf_block(t, h, 2 - core), 2, 1, -turn)
-        zf_send_to(t, h, zf_block(t, h, 5 + core), 3, 2, turn)
-        zf_send_to(t, h, zf_block(t, h, 6 - core), 4, 2, -turn)
+        zf_send_to(t, h, zf_block(t, h, 1), 1, 0, turn)
+        zf_send_to(t, h, zf_block(t, h, 2), 2, 1, -turn)
+        zf_send_to(t, h, zf_block(t, h, 3), 3, 2, turn)
+        zf_send_to(t, h, zf_block(t, h, 4), 4, 2, -turn)
 
     def zf_wait(t, h, lo, n, sem):
         arrived = zfrecv.at[t, h, pl.ds(lo, n)]
@@ -179,17 +184,17 @@
 
     def zf_mid(t, h):
         zf_wait(t, h, 0, 2, 0)
-        total = zf_own(t, h, 3 + core) + zfrecv[t, h, 0].astype(jnp.float32) + zfrecv[t, h, 1].astype(jnp.float32)
+        total = zf_own(t, h, 6) + zfrecv[t, h, 0].astype(jnp.float32) + zfrecv[t, h, 1].astype(jnp.float32)
         zfmid[t, h, 0] = total.astype(jnp.bfloat16)
         zf_send_to(t, h, zfmid.at[t, h, 0], 5, 2, 2 * turn)
         zf_wait(t, h, 2, 1, 1)
-        total = zf_own(t, h, 4 - core) + zfrecv[t, h, 2].astype(jnp.float32)
+        total = zf_own(t, h, 7) + zfrecv[t, h, 2].astype(jnp.float32)
         zfmid[t, h, 1] = total.astype(jnp.bfloat16)
         zf_send_to(t, h, zfmid.at[t, h, 1], 6, 2, -2 * turn)
 
     def zf_end(t, h):
         zf_wait(t, h, 3, 4, 2)
-        total = zf_own(t, h, nz - 1)
+        total = zf_own(t, h, OWN)
         for slot in range(3, 7):
             total += zfrecv[t, h, slot].astype(jnp.float32)
         xfsend[t, h] = total.astype(jnp.bfloat16)
@@ -197,11 +202,10 @@
             remote(xfsend.at[t, h, lax.rem(x + e, nx)], xfrecv.at[t, h, e - 1], xf_send.at[t, h], xf_recv.at[t, h], at_x(e)).start()
 
     def finish(t, h):
-        arrived = zrecv.at[t, h]
-        remote(arrived, arrived, z_send.at[t, h], z_recv.at[t, h], sibling).wait_recv()
+        z_wait(t, h, 3, 4, 2)
         total = zown[t, h]
-        for k in range(nz - 1):
-            total += zrecv[t, h, k].astype(jnp.float32)
+        for slot in range(3, 7):
+            total += zrecv[t, h, slot].astype(jnp.float32)
         lanes = slice(h * LANES, (h + 1) * LANES)
 
         def store(part_rows, total):
@@ -227,7 +231,7 @@
         some = xrecv.at[t, h]
         remote(some, some, x_send.at[t, h], x_recv.at[t, h, 0], sibling).wait_send()
         some = zsend.at[t, h]
-        remote(some, some, z_send.at[t, h], z_recv.at[t, h], sibling).wait_send()
+        remote(some, some, z_send.at[t, h], z_recv.at[t, h, 0], sibling).wait_send()
         some = zfrecv.at[t, h]
         remote(some, some, zf_send.at[t, h], zf_recv.at[t, h, 0], sibling).wait_send()
         some = xfrecv.at[t, h]
@@ -355,7 +359,7 @@
                 dma(both),
                 dma((*both, nz)),
                 dma(both),
-                dma(both),
+                dma((*both, 3)),
                 dma(both),
                 dma((*both, 3)),
                 dma(both),

time: 80.6 us -> 79.9 us (level)
  Pallas kernels: 78.2 us -> 76.9 us
    pallas_call x1, Pallas kernels: 78.2 us -> 76.9 us  [body(): pl.pallas_call(functools.partial(kernel, nx, ny, nz), out_shape=jax.Shape...]
where the time goes in v4:
time: 79.9 us; the launch traced here: 79.1 us
  Pallas kernels  76.9 us (96%)
  local copies, waits for them, and re-layouts  1.57 us (2%)
    pallas_call x1, Pallas kernels, body(): pl.pallas_call(functools.partial(kernel, nx, ny, nz), out_shape=jax.Shape...  76.9 us

profile of v4, /device:TPU:1, one launch (start us, length us, event | category | flops | bytes accessed | tf_op | source)
XLA Modules:
  0.0 79.1 jit_solution(16105646616310682908)
XLA Ops:
  0.7 76.9 %propagate.1 = f32[128,256]{1,0:T(8,128)} custom-call(bf16[1,1,128,128,128]{4,3,2,1,0:T(8,128)(2,1)} %refs_0_.1, s32[1,1,128]{2,1,0:T(1,128)} %refs_1_.1, s32[1,1,128]{2,1,0:T(1,128)} %refs_2_.1, s32[1,1]{1,0:T(1,128)S(6)} %copy.7.refs_3_, f32[128,256]{1,0:T(8,128)} %refs_4_.1), custom_call_target="tpu_custom_call" | custom-call | tf_op jit(solution)/shard_map/propagate/pallas_call | solution.py:326
  77.6 1.6 %copy.8 = f32[128,256]{1,0:T(8,128)} copy(f32[128,256]{1,0:T(8,128)} %propagate.1) | data formatting | bytes 262144

commit v5 on v4

--- a/solution.py
+++ b/solution.py
@@ -273,10 +273,10 @@
     products(0, 0)
     open_all(0, 0)
     gather_mid(0, 1)
+    gather_finish(0, 1)
+    products(0, 1)
     x_run(0, 0, 0, 1)
     zf_mid(0, 0)
-    gather_finish(0, 1)
-    products(0, 1)
     open_all(0, 1)
     x_run(0, 0, 1, groups)
     zf_end(0, 0)
@@ -304,9 +304,9 @@
     zf_end(1, 0)
     x_run(1, 1, 0, 1)
     zf_mid(1, 1)
-    finish(1, 0)
     x_run(1, 1, 1, groups)
     zf_end(1, 1)
+    finish(1, 0)
     sent(1, 0)
     finish(1, 1)
     sent(1, 1)

time: 79.9 us -> 78.9 us (0.987)
  the two profiles are of different devices: /device:TPU:1 before, /device:TPU:2 now
where the time goes in v5:
time: 78.9 us; the launch traced here: 78.8 us
  Pallas kernels  76.5 us (97%)
  local copies, waits for them, and re-layouts  1.57 us (2%)
    pallas_call x1, Pallas kernels, body(): pl.pallas_call(functools.partial(kernel, nx, ny, nz), out_shape=jax.Shape...  76.5 us

profile of v5, /device:TPU:2, one launch (start us, length us, event | category | flops | bytes accessed | tf_op | source)
XLA Modules:
  0.0 78.8 jit_solution(18201118268050956514)
XLA Ops:
  0.7 76.5 %propagate.1 = f32[128,256]{1,0:T(8,128)} custom-call(bf16[1,1,128,128,128]{4,3,2,1,0:T(8,128)(2,1)} %refs_0_.1, s32[1,1,128]{2,1,0:T(1,128)} %refs_1_.1, s32[1,1,128]{2,1,0:T(1,128)} %refs_2_.1, s32[1,1]{1,0:T(1,128)S(6)} %copy.7.refs_3_, f32[128,256]{1,0:T(8,128)} %refs_4_.1), custom_call_target="tpu_custom_call" | custom-call | tf_op jit(solution)/shard_map/propagate/pallas_call | solution.py:326
  77.2 1.6 %copy.8 = f32[128,256]{1,0:T(8,128)} copy(f32[128,256]{1,0:T(8,128)} %propagate.1) | data formatting | bytes 262144
